TPU v7x, 32 devices: a whole 2x2x4 slice. The times are simulated.
32 devices in a mesh: lon: 8 (over y, x, core), lat: 4 (over z).
Axes of the slice: x: 2, y: 2, z: 4, core: 2. Of those that a mesh axis runs over, the one named last changes fastest.
Arguments:
- heat_content_field: float32 [12, 384, 1024], P(None, 'lat', 'lon'), may hold values from -6 to 6
- saltiness_field: float32 [12, 384, 1024], P(None, 'lat', 'lon'), may hold values from -6 to 6
- eastward_cfl_number: float32 [12, 384, 1024], P(None, 'lat', 'lon'), may hold values from -0.4 to 0.4
- northward_cfl_number: float32 [12, 384, 1024], P(None, 'lat', 'lon'), may hold values from -0.4 to 0.4
- seawater_indicator: int32 [384, 1024], P('lat', 'lon'), may hold values 0 or 1
- submerged_layer_total: int32 [384, 1024], P('lat', 'lon'), may hold values from 1 to 12
- seam_partner_index: int32 [1024], replicated, may hold values from 0 to 1023, as said below
Outputs:
- new_temperature: float32 [12, 384, 1024], P(None, 'lat', 'lon')
- new_salinity: float32 [12, 384, 1024], P(None, 'lat', 'lon')
Inputs may be any that keep to these rules, and one draw needn't show every extreme that they name: Each column appears once; the map is a reflection of the columns about a pivot, seam_partner_index[i] = (s - i) mod 1024.
All inputs are finite; a program needn't handle non-finite values. No bound on the sum of `seawater_indicator` on one device may be relied on, other than what follows from the above.
Results may differ from a plain program's by a relative error of at most 0.0003.
Values sent between devices are 32-bit elements; how exact they have to be, the bound alone decides.
No kernel may reach another device: no remote copies, remote signals or barrier semaphores. Data moves between devices by JAX's collectives and lax.ppermute only.
A program may use at most 192 MiB of HBM per device.

v0:
```python
import functools

import jax
import jax.numpy as jnp
from jax import lax
from jax.experimental import pallas as pl
from jax.experimental.pallas import tpu as pltpu
from jax.sharding import PartitionSpec as P

RATIO_FLOOR = 0.05
DIFFUSIVITY = 0.1
THERMAL_COEF = 0.2
HALINE_COEF = 0.8

UNROLL = 6
HALO = 4
SUB = 8
LANES = 128


def sublanes():
    return lax.broadcasted_iota(jnp.int32, (SUB, LANES), 0)


def lanes():
    return lax.broadcasted_iota(jnp.int32, (SUB, LANES), 1)


def half_turn(tile):
    return pltpu.roll(tile, 4, 0)


def as_mask(flag):
    return (jnp.zeros((SUB, LANES), jnp.int32) + flag) > 0


def wet_count(indicator, total):
    return jnp.where(indicator == 1, total, 0).astype(jnp.float32)


def pack_rows(levels, width, seam, *refs):
    south, north, (ind_s, ind_n, tot_s, tot_n), (first, second, turn) = refs[:4], refs[4:8], refs[8:12], refs[12:]
    turn[0] = lax.div(seam[0], width)
    lat = lax.axis_index("lat")
    odd = as_mask(lat % 2)
    upper = sublanes() >= HALO
    for i in range(2 * levels):
        f, k = divmod(i, levels)
        low = jnp.where(upper, half_turn(south[f + 2][k]), south[f][k])
        high = jnp.where(upper, north[f][k], half_turn(north[f + 2][k]))
        first[i] = jnp.where(odd, low, high)
        second[i] = jnp.where(odd, high, low)
    low = wet_count(ind_s[...], tot_s[...])
    high = wet_count(ind_n[...], tot_n[...])
    first[2 * levels] = jnp.where(odd, low, high)
    second[2 * levels] = jnp.where(odd, high, low)

    @pl.when(lat == lax.axis_size("lat") - 1)
    def _():
        for i in range(2 * levels):
            f, k = divmod(i, levels)
            for j in range(HALO):
                second[i, j : j + 1, :] = north[f][k, 7 - j : 8 - j, :]
                row = 7 - j if f == 0 else (6, 5, 4, 7)[j]
                second[i, HALO + j : HALO + j + 1, :] = -north[f + 2][k, row : row + 1, :]
        for j in range(HALO):
            second[2 * levels, j : j + 1, :] = wet_count(ind_n[7 - j : 8 - j, :], tot_n[7 - j : 8 - j, :])


def stretch(levels, rows):
    blocks = LANES // levels
    stride = -(-(rows + 2 * HALO) // blocks)
    return blocks, stride, blocks * stride, -(-(HALO + stride * LANES) // SUB) * SUB


def turn_fields(levels, rows, seam, *refs):
    fields, ind, tot, block, q1, q2, q3, turned, to_east, to_west, flat, north_halo, spare = refs[:4], *refs[4:]
    blocks, stride, period, length = stretch(levels, rows)
    half = 2 * levels
    nl = lax.axis_size("lon")
    lat = lax.axis_index("lat")
    odd = as_mask(lat % 2)
    closed = as_mask((lat == 0).astype(jnp.int32))
    lane = lanes()
    upper = sublanes() >= HALO

    def south_halo(i):
        return jnp.where(closed, 0.0, jnp.where(odd, q1[i], q2[i]))

    for i in range(half + 1):
        north_halo[i] = jnp.where(odd, q2[i], q1[i])

    @pl.when(lat == lax.axis_size("lat") - 1)
    def _():
        r = seam[0] & (LANES - 1)
        at_home = lax.rem(lax.div(seam[0], LANES) - 2 * lax.axis_index("lon") + 2 * nl, nl)
        first_own = as_mask((at_home == 0).astype(jnp.int32))
        second_own = as_mask((at_home == 1).astype(jnp.int32))
        for i in range(half + 1):
            at = r - lane - jnp.where(upper, 1 if i < levels else 0, 0)
            index = at & (LANES - 1)

            def pick(tile):
                return jnp.take_along_axis(tile, index, axis=1, mode="promise_in_bounds")

            here = pick(jnp.where(first_own, block[i], q2[i]))
            north_halo[i] = jnp.where(at < 0, pick(jnp.where(second_own, block[i], q3[i])), here)

    tiles = rows // SUB
    for f in range(4):

        def fill(k, carry):
            at = HALO + HALO + k * period
            for t in range(tiles):
                flat[f, pl.ds(at + t * SUB, SUB), :] = fields[f][k, t * SUB : t * SUB + SUB, :]
            i = (f % 2) * levels + k
            n_tile, s_tile = north_halo[i], south_halo(i)
            if f >= 2:
                n_tile, s_tile = half_turn(n_tile), half_turn(s_tile)
            flat[f, pl.ds(at - SUB, SUB), :] = jnp.where(upper, s_tile, 0.0)
            flat[f, pl.ds(at + rows, SUB), :] = jnp.where(upper, 0.0, n_tile)
            return carry

        lax.fori_loop(0, levels, fill, 0, unroll=4)
    for t in range(tiles + 2):
        if t == 0:
            n = jnp.where(upper, south_halo(half), 0.0)
        elif t == tiles + 1:
            n = jnp.where(upper, 0.0, north_halo[half])
        else:
            n = wet_count(ind[t * SUB - SUB : t * SUB, :], tot[t * SUB - SUB : t * SUB, :])

        def left_over(k, carry):
            flat[4, pl.ds(HALO + HALO + k * period + (t - 1) * SUB, SUB), :] = n - k.astype(jnp.float32)
            return carry

        lax.fori_loop(0, levels, left_over, 0, unroll=4)
    end = levels * period
    for f in range(5):
        for t in range(end // SUB * SUB, length, SUB):
            keep = sublanes() + t < end
            flat[f, t : t + SUB, :] = jnp.where(keep, flat[f, t : t + SUB, :], 0.0)

    for t in range(stride):
        for f in range(5):
            turned[f, t] = flat.at[f][pl.ds(HALO + t, LANES, stride=stride), :].T

    places = [(f, t) for f in range(5) for t in range(stride)]
    first = (len(places) + 1) // 2
    for i in range(first):
        f, t = places[i]
        west, east = turned[f, t, 0:SUB, :], turned[f, t, LANES - SUB : LANES, :]
        if i + first < len(places):
            f, t = places[i + first]
            west = jnp.where(upper, half_turn(turned[f, t, 0:SUB, :]), west)
            east = jnp.where(upper, east, half_turn(turned[f, t, LANES - SUB : LANES, :]))
        to_west[i] = west
        to_east[i] = east


def ahead(tiles):
    return tiles[1:] + [pltpu.roll(tiles[0], LANES - 1, 1)]


def behind(tiles):
    return [pltpu.roll(tiles[-1], 1, 1)] + tiles[:-1]


def each(function, *lists):
    return [function(*items) for items in zip(*lists)]


def pairs(function, *lists):
    return tuple(map(list, zip(*each(function, *lists))))


def replaced(tiles, other):
    return [other.get(t, x) for t, x in enumerate(tiles)]


def flux_pair(q, q_next, half_speed, half_size):
    anti = half_size * (q_next - q)
    return half_speed * (q_next + q) - anti, anti


def limited_flux(anti, plus, minus, plus_next, minus_next):
    return anti * jnp.where(anti >= 0.0, jnp.minimum(plus_next, minus), jnp.minimum(plus, minus_next))


def reciprocal(x):
    return pl.reciprocal(x, approx=True)


def halves(speed, mask):
    half = jnp.where(mask > 0.0, 0.5 * speed, 0.0)
    return half, jnp.abs(half)


def net(q, a, b, c, d):
    return q - ((a - b) + (c - d))


def ratios(a, b, c, l, sa, sb, sc, sl):
    inflow = (jnp.maximum(b, 0.0) - jnp.minimum(a, 0.0)) + (jnp.maximum(l, 0.0) - jnp.minimum(c, 0.0))
    outflow = (jnp.maximum(a, 0.0) - jnp.minimum(b, 0.0)) + (jnp.maximum(c, 0.0) - jnp.minimum(l, 0.0))
    rise = jnp.maximum(jnp.maximum(jnp.maximum(sa, sc), 0.0), -jnp.minimum(sb, sl))
    drop = jnp.maximum(jnp.maximum(jnp.maximum(sb, sl), 0.0), -jnp.minimum(sa, sc))
    plus = jnp.minimum(1.0, rise * reciprocal(jnp.maximum(inflow, RATIO_FLOOR)))
    minus = jnp.minimum(1.0, drop * reciprocal(jnp.maximum(outflow, RATIO_FLOOR)))
    return plus, minus


def face(t0, t1, s0, s1, zt0, zt1, zs0, zs1, m):
    dt, ds, zt, zs = t1 - t0, s1 - s0, zt1 + zt0, zs1 + zs0
    bottom = jnp.maximum(HALINE_COEF * zs - THERMAL_COEF * zt, 1.0)
    half_slope = (HALINE_COEF * ds - THERMAL_COEF * dt) * reciprocal(bottom)
    half_slope = jnp.maximum(jnp.minimum(half_slope, 1.0), -1.0)
    return jnp.where(m > 0.0, dt - half_slope * zt, 0.0), jnp.where(m > 0.0, ds - half_slope * zs, 0.0)


def step(levels, rows, *refs):
    (
        turned, from_east, from_west, temp_out, salt_out,
        body, result, flat, out, sems, *grid
    ) = refs
    grid, alts, prev = grid[:17], grid[17:19], grid[19:]
    blocks, stride, period, length = stretch(levels, rows)
    columns = LANES + 2 * HALO
    nc = columns // SUB
    ts = range(stride)
    lat = lax.axis_index("lat")
    tops = as_mask((lat == lax.axis_size("lat") - 1).astype(jnp.int32))
    lane = lanes()
    upper = sublanes() >= HALO
    loads = [
        pltpu.make_async_copy(turned.at[f], body.at[f, :, 0:LANES, :], sems.at[f]) for f in range(5)
    ]
    for load in loads:
        load.start()
    places = [(f, t) for f in range(5) for t in ts]
    first = (len(places) + 1) // 2
    for i in range(first):
        f, t = places[i]
        body[f, t, LANES:columns, :] = jnp.where(upper, from_west[i], from_east[i])
        if i + first < len(places):
            f, t = places[i + first]
            body[f, t, LANES:columns, :] = half_turn(jnp.where(upper, from_east[i], from_west[i]))
    for load in loads:
        load.wait()
    for f in range(5):
        for t in ts:
            body[f, t, columns : columns + SUB, :] = body[f, t, 0:SUB, :]

    def cells(f, c):
        return [body.at[f, t][pl.ds(c, SUB, stride=nc), :] for t in ts]

    def get(place, c):
        return [grid[place][c + 1, t] for t in ts]

    def put(place, c, tiles):
        for t in ts:
            grid[place][c + 1, t] = tiles[t]

    def sweep(before, column):
        def store(lists):
            for ref, tiles in zip(prev, lists):
                for t in ts:
                    ref[t] = tiles[t]

        def some(start, count):
            lists = [[ref[t] for t in ts] for ref in prev]
            for i in range(count):
                lists = column(start + i, lists)
            store(lists)

        def body(i, carry):
            some(i * UNROLL, UNROLL)
            return carry

        store(before)
        lax.fori_loop(0, nc // UNROLL, body, 0)
        if nc % UNROLL:
            some(nc - nc % UNROLL, nc % UNROLL)

    def down(tiles):
        return [pltpu.roll(x, 1, 0) for x in tiles]

    def wrap(place, left=True, right=True):
        if left:
            put(place, -1, down(get(place, nc - 1)))
        if right:
            put(place, nc, [pltpu.roll(x, SUB - 1, 0) for x in get(place, 0)])

    seam_tile = (rows + HALO - 1) % stride
    seam_block = (rows + HALO - 1) // stride
    spare_tile = (rows + 2 * HALO - 1) % stride
    at_seam = (lane % blocks == seam_block) & tops

    def across_flux(c):
        open_c = each(jnp.minimum, cells(4, c), cells(4, c + 1))
        speed = pairs(halves, cells(2, c), open_c)
        return open_c, [pairs(flux_pair, cells(f, c), cells(f, c + 1), *speed) for f in range(2)]

    open_c, flux_c = across_flux(nc - 1)
    put(15, -1, down(open_c))
    for f in range(2):
        put(4 + f, -1, down(flux_c[f][1]))

    before = [down(low) for low, _ in flux_c]

    def upwind_step(c, old):
        open_c, flux_c = across_flux(c)
        m = cells(4, c)
        open_a = each(jnp.minimum, m, ahead(m))
        v = cells(3, c)
        speed = pairs(halves, v, open_a)
        alt = halves(jnp.where(at_seam, v[spare_tile], v[seam_tile]), open_a[seam_tile])
        results = []
        for f in range(2):
            q = cells(f, c)
            q_a = ahead(q)
            low_a, anti_a = pairs(flux_pair, q, q_a, *speed)
            low_alt, anti_alt = flux_pair(q[seam_tile], q_a[seam_tile], *alt)
            low_b = behind(replaced(low_a, {seam_tile: low_alt}))
            low_c, anti_c = flux_c[f]
            results.append((each(net, q, low_a, low_b, low_c, old[f]), anti_a, anti_c, low_c, anti_alt))
        put(14, c, open_a)
        put(15, c, open_c)
        put(16, c, m)
        for f, (upwind, anti_a, anti_c, low_c, anti_alt) in enumerate(results):
            put(f, c, upwind)
            put(2 + f, c, anti_a)
            put(4 + f, c, anti_c)
            alts[f][c] = anti_alt
        return [x[3] for x in results]

    sweep(before, upwind_step)
    wrap(0)
    wrap(1)

    def across_step(f, c):
        return each(lambda u, n, m: jnp.where(m > 0.0, n - u, 0.0), get(f, c), get(f, c + 1), get(15, c))

    def ratio_step(c, old):
        open_a = get(14, c)
        results = []
        for f in range(2):
            up = get(f, c)
            step_a = each(lambda u, n, m: jnp.where(m > 0.0, n - u, 0.0), up, ahead(up), open_a)
            step_c = across_step(f, c)
            anti_a = get(2 + f, c)
            anti_b = behind(replaced(anti_a, {seam_tile: alts[f][c]}))
            plus, minus = pairs(
                ratios, anti_a, anti_b, get(4 + f, c), get(4 + f, c - 1),
                step_a, behind(step_a), step_c, old[f],
            )
            results.append((plus, minus, step_c))
        for f, (plus, minus, step_c) in enumerate(results):
            put(6 + f, c, plus)
            put(8 + f, c, minus)
        return [x[2] for x in results]

    sweep([across_step(f, -1) for f in range(2)], ratio_step)
    for place in range(6, 10):
        wrap(place)

    def across_limited(f, c):
        return each(limited_flux, get(4 + f, c), get(6 + f, c), get(8 + f, c), get(6 + f, c + 1), get(8 + f, c + 1))

    def advect_step(c, old):
        m = get(16, c)
        results = []
        for f in range(2):
            plus, minus = get(6 + f, c), get(8 + f, c)
            plus_a, minus_a = ahead(plus), ahead(minus)
            lim_a = each(limited_flux, get(2 + f, c), plus, minus, plus_a, minus_a)
            s = seam_tile
            lim_alt = limited_flux(alts[f][c], plus[s], minus[s], plus_a[s], minus_a[s])
            lim_c = across_limited(f, c)
            new = each(net, get(f, c), lim_a, behind(replaced(lim_a, {s: lim_alt})), lim_c, old[f])
            step = each(lambda x, n: jnp.where(n > 1.0, pltpu.roll(x, LANES - blocks, 1) - x, 0.0), new, m)
            results.append((new, step, lim_c))
        for f, (new, step, lim_c) in enumerate(results):
            put(10 + f, c, new)
            put(12 + f, c, step)
        return [x[2] for x in results]

    sweep([across_limited(f, -1) for f in range(2)], advect_step)
    for place in range(10, 14):
        wrap(place)

    def across_face(c):
        sides = [get(place, at) for place in (10, 11, 12, 13) for at in (c, c + 1)]
        return pairs(face, *sides, get(15, c))

    def diffuse_step(c, old):
        values = [get(place, c) for place in (10, 11, 12, 13)]
        sides = [side for x in values for side in (x, ahead(x))]
        flux_a = pairs(face, *sides, get(14, c))
        flux_c = across_face(c)
        new = [
            each(
                lambda q, a, b, x, y: q + DIFFUSIVITY * ((a - b) + (x - y)),
                values[f], flux_a[f], behind(flux_a[f]), flux_c[f], old[f],
            )
            for f in range(2)
        ]
        for f in range(2):
            for t in ts:
                result.at[f, t][pl.ds(c, SUB, stride=nc), :] = new[f][t]
        return flux_c

    sweep(across_face(-1), diffuse_step)

    stores = []
    for f, ref in enumerate((temp_out, salt_out)):

        for t in ts:
            flat.at[f][pl.ds(HALO + t, LANES, stride=stride), :] = result[f, t, 0:LANES, :].T

        def collect(k, carry):
            for t in range(rows // SUB):
                at = HALO + HALO + k * period + t * SUB
                out[f, k, t * SUB : t * SUB + SUB, :] = flat[f, pl.ds(at, SUB), :]
            return carry

        lax.fori_loop(0, levels, collect, 0, unroll=4)
        store = pltpu.make_async_copy(out.at[f], ref, sems.at[f])
        store.start()
        stores.append(store)
    for store in stores:
        store.wait()


def local(nl, nlat, temp, salt, east, north, indicator, total, seam):
    levels, rows, width = temp.shape
    half = 2 * levels
    blocks, stride, period, length = stretch(levels, rows)
    vmem = pl.BlockSpec(memory_space=pltpu.VMEM)
    smem = pl.BlockSpec(memory_space=pltpu.SMEM)
    anywhere = pl.BlockSpec(memory_space=pl.ANY)
    f32 = jnp.float32

    def params(mib):
        return pltpu.CompilerParams(vmem_limit_bytes=mib * 1024 * 1024)

    last = rows // SUB - 1
    low = pl.BlockSpec((levels, SUB, width), lambda i: (0, 0, 0))
    high = pl.BlockSpec((levels, SUB, width), lambda i: (0, last, 0))
    flat_low = pl.BlockSpec((SUB, width), lambda i: (0, 0))
    flat_high = pl.BlockSpec((SUB, width), lambda i: (last, 0))
    block = jax.ShapeDtypeStruct((half + 1, SUB, width), f32)
    whole_block = pl.BlockSpec((half + 1, SUB, width), lambda i: (0, 0, 0))
    fields = (temp, salt, east, north)
    first, second, turn = pl.pallas_call(
        functools.partial(pack_rows, levels, width),
        grid=(1,),
        in_specs=[smem] + [low] * 4 + [high] * 4 + [flat_low, flat_high] * 2,
        out_specs=[whole_block] * 2 + [smem],
        out_shape=[block] * 2 + [jax.ShapeDtypeStruct((1,), jnp.int32)],
        compiler_params=params(56),
    )(seam, *fields, *fields, indicator, indicator, total, total)

    q1 = lax.ppermute(first, "lat", [(j, j ^ 1) for j in range(nlat)])

    def meet(turned):
        def facing(back):
            pairs = []
            for i in range(nl):
                to = (turned - back - i) % nl
                to = (i + nl // 2) % nl if to == i else to
                pairs.append((i * nlat + nlat - 1, to * nlat + nlat - 1))
            return pairs

        def idle(rows):
            return [(i * nlat + j, (i ^ 1) * nlat + j) for i in range(nl) for j in rows]

        inner = [(i * nlat + j, i * nlat + (j + 1 if j % 2 else j - 1)) for i in range(nl) for j in range(1, nlat - 1)]

        def send(x):
            return (
                lax.ppermute(x, ("lon", "lat"), idle([0]) + inner + facing(0)),
                lax.ppermute(x, ("lon", "lat"), idle(range(nlat - 1)) + facing(1)),
            )

        return send

    q2, q3 = lax.switch(turn[0], [meet(t) for t in range(nl)], second)

    payload = jax.ShapeDtypeStruct(((5 * stride + 1) // 2, SUB, width), f32)
    turned, to_east, to_west = pl.pallas_call(
        functools.partial(turn_fields, levels, rows),
        in_specs=[smem] + [vmem] * 10,
        out_specs=[vmem] * 3,
        out_shape=[jax.ShapeDtypeStruct((5, stride, width, LANES), f32), payload, payload],
        scratch_shapes=[
            pltpu.VMEM((5, length, width), f32),
            pltpu.VMEM((half + 1, SUB, width), f32),
            pltpu.VMEM((SUB, width), f32),
        ],
        compiler_params=params(20),
    )(seam, *fields, indicator, total, second, q1, q2, q3)
    from_west = lax.ppermute(to_east, "lon", [(i, (i + 1) % nl) for i in range(nl)])
    from_east = lax.ppermute(to_west, "lon", [((i + 1) % nl, i) for i in range(nl)])

    columns = width + 2 * HALO
    nc = columns // SUB
    return pl.pallas_call(
        functools.partial(step, levels, rows),
        in_specs=[anywhere, vmem, vmem],
        out_specs=[anywhere] * 2,
        out_shape=[jax.ShapeDtypeStruct(temp.shape, f32)] * 2,
        scratch_shapes=[
            pltpu.VMEM((5, stride, columns + SUB, LANES), f32),
            pltpu.VMEM((2, stride, columns, LANES), f32),
            pltpu.VMEM((2, length, width), f32),
            pltpu.VMEM((2, levels, rows, width), f32),
            pltpu.SemaphoreType.DMA((5,)),
        ]
        + [pltpu.VMEM((nc + 2, stride, SUB, LANES), f32)] * 17
        + [pltpu.VMEM((nc, SUB, LANES), f32)] * 2
        + [pltpu.VMEM((stride, SUB, LANES), f32)] * 2,
        compiler_params=params(40),
    )(turned, from_east, from_west)


def solution(mesh):
    in_specs = (
        P(None, "lat", "lon"),
        P(None, "lat", "lon"),
        P(None, "lat", "lon"),
        P(None, "lat", "lon"),
        P("lat", "lon"),
        P("lat", "lon"),
        P(),
    )
    out_specs = (P(None, "lat", "lon"), P(None, "lat", "lon"))
    body = functools.partial(local, mesh.shape["lon"], mesh.shape["lat"])
    return jax.shard_map(body, mesh=mesh, in_specs=in_specs, out_specs=out_specs, check_vma=False)
```

profile of v0, /device:TPU:24, one launch (start us, length us, event | category | flops | bytes accessed | tf_op | source)
XLA Modules:
  0.0 29.3 jit_solution(14515703777120271895)
XLA Ops:
  0.6 0.0 copy-start.6
  0.6 0.0 copy-start.5
  0.7 0.0 copy-start.4
  0.7 0.0 copy-start.3
  0.7 0.0 copy-start.2
  0.7 0.0 copy-start.1
  0.7 0.0 copy-start
  0.7 1.9 %shard_map.86 = (f32[25,8,128]{2,1,0:T(8,128)}, f32[25,8,128]{2,1,0:T(8,128)S(1)}, s32[1]{0:T(128)}) custom-call(s32[1024]{0:T(1024)} %seam.3, f32[12,96,128]{2,1,0:T(8,128)} %refs_0_.3, f32[12,96,128]{2,1,0:T(8,128)} %refs_1_.3, f32[12,96,128]{2,1,0:T(8,128)} %refs_2_.3, f32[12,96,128]{2,1,0:T(8,128)} %refs_3_.3, f32[12,96,128]{2,1,0:T(8,128)} %refs_0_.3, ...), custom_call_target="tpu_custom_call" | custom-call | tf_op jit(solution)/shard_map/pallas_call | solution.py:455
  2.6 0.4 %collective-permute-start.16 = (f32[25,8,128]{2,1,0:T(8,128)}, f32[25,8,128]{2,1,0:T(8,128)S(1)}, u32[]{:S(2)}, u32[]{:S(2)}) collective-permute-start(f32[25,8,128]{2,1,0:T(8,128)} %get-tuple-element.19), channel_id=1, source_target_pairs={{0,1},{1,0},{2,3},{3,2},{4,5},{5,4},{6,7},{7,6},{8,9},{9,8},{10,11... | collective-permute-start | bytes 307208 | tf_op jit(solution)/shard_map/ppermute | solution.py:464
  3.7 8.0 %conditional.1 = (f32[25,8,128]{2,1,0:T(8,128)}, f32[25,8,128]{2,1,0:T(8,128)}) conditional(s32[]{:T(128)} %bitcast, f32[25,8,128]{2,1,0:T(8,128)S(1)} %get-tuple-element.18.refs_6_, f32[25,8,128]{2,1,0:T(8,128)S(1)} %get-tuple-element.18.refs_6_, f32[25,8,128]{2,1,0:T(8,128)S(1)} %get-tuple-element.18.refs_6_, ...), branch_computations={%region_0.0_spmd, %region_1.0_spmd, %region_2.0_spmd, %region_3.0_... | conditional | bytes 819296 | solution.py:488
  3.7 2.5 %collective-permute-start.15 = (f32[25,8,128]{2,1,0:T(8,128)S(1)}, f32[25,8,128]{2,1,0:T(8,128)}, u32[]{:S(2)}, u32[]{:S(2)}) collective-permute-start(f32[25,8,128]{2,1,0:T(8,128)S(1)} %param.7), channel_id=1, source_target_pairs={{0,4},{1,5},{2,6},{4,0},{5,1},{6,2},{8,12},{9,13},{10,14},{12,8},{... | collective-permute-start | bytes 307208 | tf_op jit(solution)/shard_map/cond/branch_7_fun/ppermute | solution.py:483
  6.2 0.0 collective-permute-start.14
  6.3 3.2 %collective-permute-done.15 = f32[25,8,128]{2,1,0:T(8,128)} collective-permute-done((f32[25,8,128]{2,1,0:T(8,128)S(1)}, f32[25,8,128]{2,1,0:T(8,128)}, u32[]{:S(2)}, u32[]{:S(2)}) %collective-permute-start.15) | collective-permute-done | bytes 102432 | tf_op jit(solution)/shard_map/cond/branch_7_fun/ppermute | solution.py:483
  9.5 2.2 %collective-permute-done.14 = f32[25,8,128]{2,1,0:T(8,128)} collective-permute-done((f32[25,8,128]{2,1,0:T(8,128)S(1)}, f32[25,8,128]{2,1,0:T(8,128)}, u32[]{:S(2)}, u32[]{:S(2)}) %collective-permute-start.14) | collective-permute-done | bytes 102432 | tf_op jit(solution)/shard_map/cond/branch_7_fun/ppermute | solution.py:482
  11.7 0.0 collective-permute-done.16.refs_7_
  11.7 0.0 copy-done.6
  11.7 0.0 copy-done.5
  11.7 0.0 copy-done.4
  11.7 0.0 copy-done.3
  11.7 0.0 copy-done.2
  11.7 0.0 copy-done.1
  11.7 0.0 copy-done
  11.7 2.7 %shard_map.87 = (f32[5,11,128,128]{3,2,1,0:T(8,128)S(1)}, f32[28,8,128]{2,1,0:T(8,128)S(1)}, f32[28,8,128]{2,1,0:T(8,128)S(1)}) custom-call(s32[1024]{0:T(1024)S(1)} %copy-done.6, f32[12,96,128]{2,1,0:T(8,128)S(1)} %copy-done, f32[12,96,128]{2,1,0:T(8,128)S(1)} %copy-done.1, f32[12,96,128]{2,1,0:T(8,128)S(1)} %copy-done.2, f32[12,96,128]{2,1,0:T(8,128)S(1)} %copy-done.3, ...), custom_call_target="tpu_custom_call" | custom-call | tf_op jit(solution)/shard_map/pallas_call | solution.py:491
  14.4 1.8 %collective-permute-start.17 = (f32[28,8,128]{2,1,0:T(8,128)S(1)}, f32[28,8,128]{2,1,0:T(8,128)S(1)}, u32[]{:S(2)}, u32[]{:S(2)}) collective-permute-start(f32[28,8,128]{2,1,0:T(8,128)S(1)} %get-tuple-element.24), channel_id=1, source_target_pairs={{4,0},{8,4},{12,8},{16,12},{20,16},{24,20},{28,24},{0,28},{5,1},{9... | collective-permute-start | bytes 344072 | tf_op jit(solution)/shard_map/ppermute | solution.py:504
  16.2 0.0 collective-permute-start.18
  16.2 2.5 %collective-permute-done.17.refs_1_ = f32[28,8,128]{2,1,0:T(8,128)S(1)} collective-permute-done((f32[28,8,128]{2,1,0:T(8,128)S(1)}, f32[28,8,128]{2,1,0:T(8,128)S(1)}, u32[]{:S(2)}, u32[]{:S(2)}) %collective-permute-start.17) | collective-permute-done | bytes 114720 | tf_op jit(solution)/shard_map/ppermute | solution.py:504
  18.8 2.6 %collective-permute-done.18.refs_2_ = f32[28,8,128]{2,1,0:T(8,128)S(1)} collective-permute-done((f32[28,8,128]{2,1,0:T(8,128)S(1)}, f32[28,8,128]{2,1,0:T(8,128)S(1)}, u32[]{:S(2)}, u32[]{:S(2)}) %collective-permute-start.18) | collective-permute-done | bytes 114720 | tf_op jit(solution)/shard_map/ppermute | solution.py:503
  21.3 7.9 %shard_map.88 = (f32[12,96,128]{2,1,0:T(8,128)}, f32[12,96,128]{2,1,0:T(8,128)}) custom-call(f32[5,11,128,128]{3,2,1,0:T(8,128)S(1)} %get-tuple-element.23.refs_0_, f32[28,8,128]{2,1,0:T(8,128)S(1)} %collective-permute-done.17.refs_1_, f32[28,8,128]{2,1,0:T(8,128)S(1)} %collective-permute-done.18.refs_2_), custom_call_target="tpu_custom_call" | custom-call | tf_op jit(solution)/shard_map/pallas_call | solution.py:508
Async XLA Ops:
  0.6 11.0 %copy-start.6 = (s32[1024]{0:T(1024)S(1)}, s32[1024]{0:T(1024)}, u32[]{:S(2)}) copy-start(s32[1024]{0:T(1024)} %seam.3) | copy-start | bytes 12292
  0.6 11.0 %copy-start.5 = (s32[96,128]{1,0:T(8,128)S(1)}, s32[96,128]{1,0:T(8,128)}, u32[]{:S(2)}) copy-start(s32[96,128]{1,0:T(8,128)} %refs_5_.3) | copy-start | bytes 147460
  0.7 11.0 %copy-start.4 = (s32[96,128]{1,0:T(8,128)S(1)}, s32[96,128]{1,0:T(8,128)}, u32[]{:S(2)}) copy-start(s32[96,128]{1,0:T(8,128)} %refs_4_.3) | copy-start | bytes 147460
  0.7 11.0 %copy-start.3 = (f32[12,96,128]{2,1,0:T(8,128)S(1)}, f32[12,96,128]{2,1,0:T(8,128)}, u32[]{:S(2)}) copy-start(f32[12,96,128]{2,1,0:T(8,128)} %refs_3_.3) | copy-start | bytes 1769476
  0.7 11.0 %copy-start.2 = (f32[12,96,128]{2,1,0:T(8,128)S(1)}, f32[12,96,128]{2,1,0:T(8,128)}, u32[]{:S(2)}) copy-start(f32[12,96,128]{2,1,0:T(8,128)} %refs_2_.3) | copy-start | bytes 1769476
  0.7 11.0 %copy-start.1 = (f32[12,96,128]{2,1,0:T(8,128)S(1)}, f32[12,96,128]{2,1,0:T(8,128)}, u32[]{:S(2)}) copy-start(f32[12,96,128]{2,1,0:T(8,128)} %refs_1_.3) | copy-start | bytes 1769476
  0.7 11.0 %copy-start = (f32[12,96,128]{2,1,0:T(8,128)S(1)}, f32[12,96,128]{2,1,0:T(8,128)}, u32[]{:S(2)}) copy-start(f32[12,96,128]{2,1,0:T(8,128)} %refs_0_.3) | copy-start | bytes 1769476
  2.6 9.0 %collective-permute-start.16 = (f32[25,8,128]{2,1,0:T(8,128)}, f32[25,8,128]{2,1,0:T(8,128)S(1)}, u32[]{:S(2)}, u32[]{:S(2)}) collective-permute-start(f32[25,8,128]{2,1,0:T(8,128)} %get-tuple-element.19), channel_id=1, source_target_pairs={{0,1},{1,0},{2,3},{3,2},{4,5},{5,4},{6,7},{7,6},{8,9},{9,8},{10,11... | collective-permute-start | bytes 307208 | tf_op jit(solution)/shard_map/ppermute | solution.py:464
  3.7 5.7 %collective-permute-start.15 = (f32[25,8,128]{2,1,0:T(8,128)S(1)}, f32[25,8,128]{2,1,0:T(8,128)}, u32[]{:S(2)}, u32[]{:S(2)}) collective-permute-start(f32[25,8,128]{2,1,0:T(8,128)S(1)} %param.7), channel_id=1, source_target_pairs={{0,4},{1,5},{2,6},{4,0},{5,1},{6,2},{8,12},{9,13},{10,14},{12,8},{... | collective-permute-start | bytes 307208 | tf_op jit(solution)/shard_map/cond/branch_7_fun/ppermute | solution.py:483
  6.2 5.4 %collective-permute-start.14 = (f32[25,8,128]{2,1,0:T(8,128)S(1)}, f32[25,8,128]{2,1,0:T(8,128)}, u32[]{:S(2)}, u32[]{:S(2)}) collective-permute-start(f32[25,8,128]{2,1,0:T(8,128)S(1)} %param.7), channel_id=1, source_target_pairs={{0,4},{4,0},{8,12},{12,8},{16,20},{20,16},{24,28},{28,24},{1,2},{2... | collective-permute-start | bytes 307208 | tf_op jit(solution)/shard_map/cond/branch_7_fun/ppermute | solution.py:482
  14.4 4.4 %collective-permute-start.17 = (f32[28,8,128]{2,1,0:T(8,128)S(1)}, f32[28,8,128]{2,1,0:T(8,128)S(1)}, u32[]{:S(2)}, u32[]{:S(2)}) collective-permute-start(f32[28,8,128]{2,1,0:T(8,128)S(1)} %get-tuple-element.24), channel_id=1, source_target_pairs={{4,0},{8,4},{12,8},{16,12},{20,16},{24,20},{28,24},{0,28},{5,1},{9... | collective-permute-start | bytes 344072 | tf_op jit(solution)/shard_map/ppermute | solution.py:504
  16.2 5.1 %collective-permute-start.18 = (f32[28,8,128]{2,1,0:T(8,128)S(1)}, f32[28,8,128]{2,1,0:T(8,128)S(1)}, u32[]{:S(2)}, u32[]{:S(2)}) collective-permute-start(f32[28,8,128]{2,1,0:T(8,128)S(1)} %get-tuple-element.25), channel_id=1, source_target_pairs={{0,4},{4,8},{8,12},{12,16},{16,20},{20,24},{24,28},{28,0},{1,5},{5... | collective-permute-start | bytes 344072 | tf_op jit(solution)/shard_map/ppermute | solution.py:503
where the time goes:
time: 28.7 us; the launch traced here: 29.3 us
  Pallas kernels  12.5 us (44%)
  waiting for transfers between devices  10.5 us (37%)
  starting transfers between devices  4.78 us (17%)
  between operations  1.4 us (5%)
    pallas_call x1, Pallas kernels, local(): pl.pallas_call(functools.partial(step, levels, rows), in_specs=[anywhere,...  7.93 us
    ppermute x1, waiting for transfers between devices, send(): lax.ppermute(x, ('lon', 'lat'), idle(range(nlat - 1)) + facing(1))  3.21 us
    pallas_call x1, Pallas kernels, local(): pl.pallas_call(functools.partial(turn_fields, levels, rows), in_specs=[sm...  2.67 us
    ppermute x1, waiting for transfers between devices, local(): lax.ppermute(to_east, 'lon', [(i, (i + 1) % nl) for i in range(nl)])  2.57 us
    ppermute x1, waiting for transfers between devices, local(): lax.ppermute(to_west, 'lon', [((i + 1) % nl, i) for i in range(nl)])  2.55 us
    ppermute x1, starting transfers between devices, send(): lax.ppermute(x, ('lon', 'lat'), idle(range(nlat - 1)) + facing(1))  2.51 us
    ppermute x1, waiting for transfers between devices, send(): lax.ppermute(x, ('lon', 'lat'), idle([0]) + inner + facing(0))  2.19 us
    pallas_call x1, Pallas kernels, local(): pl.pallas_call(functools.partial(pack_rows, levels, width), grid=(1,), in...  1.91 us
  transfers between devices with their start and end apart: 5, of which 4 were waited for; matrix products, arithmetic and copies ran while one was open for 0% of the time, Pallas kernels for 0%

commit v1 on v0

--- a/solution.py
+++ b/solution.py
@@ -12,6 +12,7 @@
 THERMAL_COEF = 0.2
 HALINE_COEF = 0.8
 
+BATCH = 3
 UNROLL = 6
 HALO = 4
 SUB = 8
@@ -121,7 +122,7 @@
             flat[f, pl.ds(at + rows, SUB), :] = jnp.where(upper, 0.0, n_tile)
             return carry
 
-        lax.fori_loop(0, levels, fill, 0, unroll=4)
+        lax.fori_loop(0, levels, fill, 0, unroll=12)
     for t in range(tiles + 2):
         if t == 0:
             n = jnp.where(upper, south_halo(half), 0.0)
@@ -134,7 +135,7 @@
             flat[4, pl.ds(HALO + HALO + k * period + (t - 1) * SUB, SUB), :] = n - k.astype(jnp.float32)
             return carry
 
-        lax.fori_loop(0, levels, left_over, 0, unroll=4)
+        lax.fori_loop(0, levels, left_over, 0, unroll=12)
     end = levels * period
     for f in range(5):
         for t in range(end // SUB * SUB, length, SUB):
@@ -251,15 +252,25 @@
         for t in ts:
             body[f, t, columns : columns + SUB, :] = body[f, t, 0:SUB, :]
 
+    held = {}
+
+    def load(key, c, tile):
+        if key + c[1:] not in held:
+            held[key + c[1:]] = [tile(sum(c), t) for t in ts]
+        return held[key + c[1:]]
+
+    def after(c, n=1):
+        return c[0], c[1] + n
+
     def cells(f, c):
-        return [body.at[f, t][pl.ds(c, SUB, stride=nc), :] for t in ts]
+        return load((f, "in"), c, lambda at, t: body.at[f, t][pl.ds(at, SUB, stride=nc), :])
 
     def get(place, c):
-        return [grid[place][c + 1, t] for t in ts]
+        return load((place,), c, lambda at, t: grid[place][at + 1, t])
 
     def put(place, c, tiles):
         for t in ts:
-            grid[place][c + 1, t] = tiles[t]
+            grid[place][sum(c) + 1, t] = tiles[t]
 
     def sweep(before, column):
         def store(lists):
@@ -268,10 +279,12 @@
                     ref[t] = tiles[t]
 
         def some(start, count):
+            held.clear()
             lists = [[ref[t] for t in ts] for ref in prev]
             for i in range(count):
-                lists = column(start + i, lists)
+                lists = column((start, i), lists)
             store(lists)
+            held.clear()
 
         def body(i, carry):
             some(i * UNROLL, UNROLL)
@@ -285,11 +298,12 @@
     def down(tiles):
         return [pltpu.roll(x, 1, 0) for x in tiles]
 
-    def wrap(place, left=True, right=True):
-        if left:
-            put(place, -1, down(get(place, nc - 1)))
-        if right:
-            put(place, nc, [pltpu.roll(x, SUB - 1, 0) for x in get(place, 0)])
+    def wrap(*places):
+        held.clear()
+        for place in places:
+            put(place, (0, -1), down(get(place, (0, nc - 1))))
+            put(place, (0, nc), [pltpu.roll(x, SUB - 1, 0) for x in get(place, (0, 0))])
+        held.clear()
 
     seam_tile = (rows + HALO - 1) % stride
     seam_block = (rows + HALO - 1) // stride
@@ -297,14 +311,14 @@
     at_seam = (lane % blocks == seam_block) & tops
 
     def across_flux(c):
-        open_c = each(jnp.minimum, cells(4, c), cells(4, c + 1))
+        open_c = each(jnp.minimum, cells(4, c), cells(4, after(c)))
         speed = pairs(halves, cells(2, c), open_c)
-        return open_c, [pairs(flux_pair, cells(f, c), cells(f, c + 1), *speed) for f in range(2)]
-
-    open_c, flux_c = across_flux(nc - 1)
-    put(15, -1, down(open_c))
+        return open_c, [pairs(flux_pair, cells(f, c), cells(f, after(c)), *speed) for f in range(2)]
+
+    open_c, flux_c = across_flux((0, nc - 1))
+    put(15, (0, -1), down(open_c))
     for f in range(2):
-        put(4 + f, -1, down(flux_c[f][1]))
+        put(4 + f, (0, -1), down(flux_c[f][1]))
 
     before = [down(low) for low, _ in flux_c]
 
@@ -331,15 +345,14 @@
             put(f, c, upwind)
             put(2 + f, c, anti_a)
             put(4 + f, c, anti_c)
-            alts[f][c] = anti_alt
+            alts[f][sum(c)] = anti_alt
         return [x[3] for x in results]
 
     sweep(before, upwind_step)
-    wrap(0)
-    wrap(1)
+    wrap(0, 1)
 
     def across_step(f, c):
-        return each(lambda u, n, m: jnp.where(m > 0.0, n - u, 0.0), get(f, c), get(f, c + 1), get(15, c))
+        return each(lambda u, n, m: jnp.where(m > 0.0, n - u, 0.0), get(f, c), get(f, after(c)), get(15, c))
 
     def ratio_step(c, old):
         open_a = get(14, c)
@@ -349,9 +362,9 @@
             step_a = each(lambda u, n, m: jnp.where(m > 0.0, n - u, 0.0), up, ahead(up), open_a)
             step_c = across_step(f, c)
             anti_a = get(2 + f, c)
-            anti_b = behind(replaced(anti_a, {seam_tile: alts[f][c]}))
+            anti_b = behind(replaced(anti_a, {seam_tile: alts[f][sum(c)]}))
             plus, minus = pairs(
-                ratios, anti_a, anti_b, get(4 + f, c), get(4 + f, c - 1),
+                ratios, anti_a, anti_b, get(4 + f, c), get(4 + f, after(c, -1)),
                 step_a, behind(step_a), step_c, old[f],
             )
             results.append((plus, minus, step_c))
@@ -360,12 +373,11 @@
             put(8 + f, c, minus)
         return [x[2] for x in results]
 
-    sweep([across_step(f, -1) for f in range(2)], ratio_step)
-    for place in range(6, 10):
-        wrap(place)
+    sweep([across_step(f, (0, -1)) for f in range(2)], ratio_step)
+    wrap(6, 7, 8, 9)
 
     def across_limited(f, c):
-        return each(limited_flux, get(4 + f, c), get(6 + f, c), get(8 + f, c), get(6 + f, c + 1), get(8 + f, c + 1))
+        return each(limited_flux, get(4 + f, c), get(6 + f, c), get(8 + f, c), get(6 + f, after(c)), get(8 + f, after(c)))
 
     def advect_step(c, old):
         m = get(16, c)
@@ -375,7 +387,7 @@
             plus_a, minus_a = ahead(plus), ahead(minus)
             lim_a = each(limited_flux, get(2 + f, c), plus, minus, plus_a, minus_a)
             s = seam_tile
-            lim_alt = limited_flux(alts[f][c], plus[s], minus[s], plus_a[s], minus_a[s])
+            lim_alt = limited_flux(alts[f][sum(c)], plus[s], minus[s], plus_a[s], minus_a[s])
             lim_c = across_limited(f, c)
             new = each(net, get(f, c), lim_a, behind(replaced(lim_a, {s: lim_alt})), lim_c, old[f])
             step = each(lambda x, n: jnp.where(n > 1.0, pltpu.roll(x, LANES - blocks, 1) - x, 0.0), new, m)
@@ -385,12 +397,11 @@
             put(12 + f, c, step)
         return [x[2] for x in results]
 
-    sweep([across_limited(f, -1) for f in range(2)], advect_step)
-    for place in range(10, 14):
-        wrap(place)
+    sweep([across_limited(f, (0, -1)) for f in range(2)], advect_step)
+    wrap(10, 11, 12, 13)
 
     def across_face(c):
-        sides = [get(place, at) for place in (10, 11, 12, 13) for at in (c, c + 1)]
+        sides = [get(place, at) for place in (10, 11, 12, 13) for at in (c, after(c))]
         return pairs(face, *sides, get(15, c))
 
     def diffuse_step(c, old):
@@ -407,27 +418,24 @@
         ]
         for f in range(2):
             for t in ts:
-                result.at[f, t][pl.ds(c, SUB, stride=nc), :] = new[f][t]
+                result.at[f, t][pl.ds(sum(c), SUB, stride=nc), :] = new[f][t]
         return flux_c
 
-    sweep(across_face(-1), diffuse_step)
+    sweep(across_face((0, -1)), diffuse_step)
 
     stores = []
     for f, ref in enumerate((temp_out, salt_out)):
-
         for t in ts:
             flat.at[f][pl.ds(HALO + t, LANES, stride=stride), :] = result[f, t, 0:LANES, :].T
-
-        def collect(k, carry):
-            for t in range(rows // SUB):
-                at = HALO + HALO + k * period + t * SUB
-                out[f, k, t * SUB : t * SUB + SUB, :] = flat[f, pl.ds(at, SUB), :]
-            return carry
-
-        lax.fori_loop(0, levels, collect, 0, unroll=4)
-        store = pltpu.make_async_copy(out.at[f], ref, sems.at[f])
-        store.start()
-        stores.append(store)
+        for g in range(0, levels, BATCH):
+            for k in range(g, g + BATCH):
+                for t in range(rows // SUB):
+                    at = HALO + HALO + k * period + t * SUB
+                    out[f, k, t * SUB : t * SUB + SUB, :] = flat[f, at : at + SUB, :]
+            levels_of = pl.ds(g, BATCH)
+            store = pltpu.make_async_copy(out.at[f, levels_of], ref.at[levels_of], sems.at[len(stores)])
+            store.start()
+            stores.append(store)
     for store in stores:
         store.wait()
 
@@ -515,7 +523,7 @@
             pltpu.VMEM((2, stride, columns, LANES), f32),
             pltpu.VMEM((2, length, width), f32),
             pltpu.VMEM((2, levels, rows, width), f32),
-            pltpu.SemaphoreType.DMA((5,)),
+            pltpu.SemaphoreType.DMA((2 * levels,)),
         ]
         + [pltpu.VMEM((nc + 2, stride, SUB, LANES), f32)] * 17
         + [pltpu.VMEM((nc, SUB, LANES), f32)] * 2

time: 28.7 us -> 28.4 us (0.990); the launches traced: 29.3 us -> 28.5 us
  waiting for transfers between devices: 10.5 us -> 8.74 us
  starting transfers between devices: 4.78 us -> 6.33 us
  Pallas kernels: 12.5 us -> 12 us
    ppermute x1, starting transfers between devices: 1.83 us -> 4.11 us  [local(): lax.ppermute(to_west, 'lon', [((i + 1) % nl, i) for i in range(nl)])]
    ppermute x1, waiting for transfers between devices: 2.19 us -> 0.01 us  [send(): lax.ppermute(x, ('lon', 'lat'), idle([0]) + inner + facing(0))]
    ppermute x1, starting transfers between devices: 2.51 us -> 1.58 us  [send(): lax.ppermute(x, ('lon', 'lat'), idle(range(nlat - 1)) + facing(1))]
    ppermute x1, waiting for transfers between devices: 3.21 us -> 3.62 us  [send(): lax.ppermute(x, ('lon', 'lat'), idle(range(nlat - 1)) + facing(1))]
    pallas_call x1, Pallas kernels: 2.67 us -> 2.28 us  [local(): pl.pallas_call(functools.partial(turn_fields, levels, rows), in_specs=[sm...]
  transfers between devices with their start and end apart: 5 -> 5, of which waited for: 4 -> 3; matrix products, arithmetic and copies ran while one was open for 0% -> 0% of each run, Pallas kernels for 0% -> 0%
where the time goes in v1:
time: 28.4 us; the launch traced here: 28.5 us
  Pallas kernels  12 us (42%)
  waiting for transfers between devices  8.74 us (31%)
  starting transfers between devices  6.33 us (22%)
  between operations  1.4 us (5%)
    pallas_call x1, Pallas kernels, local(): pl.pallas_call(functools.partial(step, levels, rows), in_specs=[anywhere,...  7.79 us
    ppermute x1, starting transfers between devices, local(): lax.ppermute(to_west, 'lon', [((i + 1) % nl, i) for i in range(nl)])  4.11 us
    ppermute x1, waiting for transfers between devices, send(): lax.ppermute(x, ('lon', 'lat'), idle(range(nlat - 1)) + facing(1))  3.62 us
    ppermute x1, waiting for transfers between devices, local(): lax.ppermute(to_east, 'lon', [(i, (i + 1) % nl) for i in range(nl)])  2.75 us
    ppermute x1, waiting for transfers between devices, local(): lax.ppermute(to_west, 'lon', [((i + 1) % nl, i) for i in range(nl)])  2.36 us
    pallas_call x1, Pallas kernels, local(): pl.pallas_call(functools.partial(turn_fields, levels, rows), in_specs=[sm...  2.28 us
    pallas_call x1, Pallas kernels, local(): pl.pallas_call(functools.partial(pack_rows, levels, width), grid=(1,), in...  1.91 us
    ppermute x1, starting transfers between devices, send(): lax.ppermute(x, ('lon', 'lat'), idle(range(nlat - 1)) + facing(1))  1.58 us
  transfers between devices with their start and end apart: 5, of which 3 were waited for; matrix products, arithmetic and copies ran while one was open for 0% of the time, Pallas kernels for 0%

profile of v1, /device:TPU:24, one launch (start us, length us, event | category | flops | bytes accessed | tf_op | source)
XLA Modules:
  0.0 28.5 jit_solution(3237494805828028006)
XLA Ops:
  0.6 0.0 copy-start.6
  0.6 0.0 copy-start.5
  0.7 0.0 copy-start.4
  0.7 0.0 copy-start.3
  0.7 0.0 copy-start.2
  0.7 0.0 copy-start.1
  0.7 0.0 copy-start
  0.7 1.9 %shard_map.86 = (f32[25,8,128]{2,1,0:T(8,128)}, f32[25,8,128]{2,1,0:T(8,128)S(1)}, s32[1]{0:T(128)}) custom-call(s32[1024]{0:T(1024)} %seam.3, f32[12,96,128]{2,1,0:T(8,128)} %refs_0_.3, f32[12,96,128]{2,1,0:T(8,128)} %refs_1_.3, f32[12,96,128]{2,1,0:T(8,128)} %refs_2_.3, f32[12,96,128]{2,1,0:T(8,128)} %refs_3_.3, f32[12,96,128]{2,1,0:T(8,128)} %refs_0_.3, ...), custom_call_target="tpu_custom_call" | custom-call | tf_op jit(solution)/shard_map/pallas_call | solution.py:463
  2.6 0.4 %collective-permute-start.16 = (f32[25,8,128]{2,1,0:T(8,128)}, f32[25,8,128]{2,1,0:T(8,128)S(1)}, u32[]{:S(2)}, u32[]{:S(2)}) collective-permute-start(f32[25,8,128]{2,1,0:T(8,128)} %get-tuple-element.19), channel_id=1, source_target_pairs={{0,1},{1,0},{2,3},{3,2},{4,5},{5,4},{6,7},{7,6},{8,9},{9,8},{10,11... | collective-permute-start | bytes 307208 | tf_op jit(solution)/shard_map/ppermute | solution.py:472
  3.7 5.4 %conditional.1 = (f32[25,8,128]{2,1,0:T(8,128)}, f32[25,8,128]{2,1,0:T(8,128)}) conditional(s32[]{:T(128)} %bitcast, f32[25,8,128]{2,1,0:T(8,128)S(1)} %get-tuple-element.18.refs_6_, f32[25,8,128]{2,1,0:T(8,128)S(1)} %get-tuple-element.18.refs_6_, f32[25,8,128]{2,1,0:T(8,128)S(1)} %get-tuple-element.18.refs_6_, ...), branch_computations={%region_0.0_spmd, %region_1.0_spmd, %region_2.0_spmd, %region_3.0_... | conditional | bytes 819296 | solution.py:496
  3.7 1.6 %collective-permute-start.3 = (f32[25,8,128]{2,1,0:T(8,128)S(1)}, f32[25,8,128]{2,1,0:T(8,128)}, u32[]{:S(2)}, u32[]{:S(2)}) collective-permute-start(f32[25,8,128]{2,1,0:T(8,128)S(1)} %param.1), channel_id=1, source_target_pairs={{0,4},{1,5},{2,6},{4,0},{5,1},{6,2},{8,12},{9,13},{10,14},{12,8},{... | collective-permute-start | bytes 307208 | tf_op jit(solution)/shard_map/cond/branch_1_fun/ppermute | solution.py:491
  5.3 0.2 collective-permute-start.2
  5.5 3.6 %collective-permute-done.3 = f32[25,8,128]{2,1,0:T(8,128)} collective-permute-done((f32[25,8,128]{2,1,0:T(8,128)S(1)}, f32[25,8,128]{2,1,0:T(8,128)}, u32[]{:S(2)}, u32[]{:S(2)}) %collective-permute-start.3) | collective-permute-done | bytes 102432 | tf_op jit(solution)/shard_map/cond/branch_1_fun/ppermute | solution.py:491
  9.1 0.0 collective-permute-done.2
  9.1 0.0 collective-permute-done.16.refs_7_
  9.1 0.0 copy-done.6
  9.2 0.0 copy-done.5
  9.2 0.0 copy-done.4
  9.2 0.0 copy-done.3
  9.2 0.0 copy-done.2
  9.2 0.0 copy-done.1
  9.2 0.0 copy-done
  9.2 2.3 %shard_map.87 = (f32[5,11,128,128]{3,2,1,0:T(8,128)S(1)}, f32[28,8,128]{2,1,0:T(8,128)S(1)}, f32[28,8,128]{2,1,0:T(8,128)S(1)}) custom-call(s32[1024]{0:T(1024)S(1)} %copy-done.6, f32[12,96,128]{2,1,0:T(8,128)S(1)} %copy-done, f32[12,96,128]{2,1,0:T(8,128)S(1)} %copy-done.1, f32[12,96,128]{2,1,0:T(8,128)S(1)} %copy-done.2, f32[12,96,128]{2,1,0:T(8,128)S(1)} %copy-done.3, ...), custom_call_target="tpu_custom_call" | custom-call | tf_op jit(solution)/shard_map/pallas_call | solution.py:499
  11.5 4.1 %collective-permute-start.17 = (f32[28,8,128]{2,1,0:T(8,128)S(1)}, f32[28,8,128]{2,1,0:T(8,128)S(1)}, u32[]{:S(2)}, u32[]{:S(2)}) collective-permute-start(f32[28,8,128]{2,1,0:T(8,128)S(1)} %get-tuple-element.24), channel_id=1, source_target_pairs={{4,0},{8,4},{12,8},{16,12},{20,16},{24,20},{28,24},{0,28},{5,1},{9... | collective-permute-start | bytes 344072 | tf_op jit(solution)/shard_map/ppermute | solution.py:512
  15.6 0.0 collective-permute-start.18
  15.6 2.4 %collective-permute-done.17.refs_1_ = f32[28,8,128]{2,1,0:T(8,128)S(1)} collective-permute-done((f32[28,8,128]{2,1,0:T(8,128)S(1)}, f32[28,8,128]{2,1,0:T(8,128)S(1)}, u32[]{:S(2)}, u32[]{:S(2)}) %collective-permute-start.17) | collective-permute-done | bytes 114720 | tf_op jit(solution)/shard_map/ppermute | solution.py:512
  18.0 2.7 %collective-permute-done.18.refs_2_ = f32[28,8,128]{2,1,0:T(8,128)S(1)} collective-permute-done((f32[28,8,128]{2,1,0:T(8,128)S(1)}, f32[28,8,128]{2,1,0:T(8,128)S(1)}, u32[]{:S(2)}, u32[]{:S(2)}) %collective-permute-start.18) | collective-permute-done | bytes 114720 | tf_op jit(solution)/shard_map/ppermute | solution.py:511
  20.7 7.8 %shard_map.88 = (f32[12,96,128]{2,1,0:T(8,128)}, f32[12,96,128]{2,1,0:T(8,128)}) custom-call(f32[5,11,128,128]{3,2,1,0:T(8,128)S(1)} %get-tuple-element.23.refs_0_, f32[28,8,128]{2,1,0:T(8,128)S(1)} %collective-permute-done.17.refs_1_, f32[28,8,128]{2,1,0:T(8,128)S(1)} %collective-permute-done.18.refs_2_), custom_call_target="tpu_custom_call" | custom-call | tf_op jit(solution)/shard_map/pallas_call | solution.py:516
Async XLA Ops:
  0.6 8.5 %copy-start.6 = (s32[1024]{0:T(1024)S(1)}, s32[1024]{0:T(1024)}, u32[]{:S(2)}) copy-start(s32[1024]{0:T(1024)} %seam.3) | copy-start | bytes 12292
  0.6 8.5 %copy-start.5 = (s32[96,128]{1,0:T(8,128)S(1)}, s32[96,128]{1,0:T(8,128)}, u32[]{:S(2)}) copy-start(s32[96,128]{1,0:T(8,128)} %refs_5_.3) | copy-start | bytes 147460
  0.7 8.5 %copy-start.4 = (s32[96,128]{1,0:T(8,128)S(1)}, s32[96,128]{1,0:T(8,128)}, u32[]{:S(2)}) copy-start(s32[96,128]{1,0:T(8,128)} %refs_4_.3) | copy-start | bytes 147460
  0.7 8.5 %copy-start.3 = (f32[12,96,128]{2,1,0:T(8,128)S(1)}, f32[12,96,128]{2,1,0:T(8,128)}, u32[]{:S(2)}) copy-start(f32[12,96,128]{2,1,0:T(8,128)} %refs_3_.3) | copy-start | bytes 1769476
  0.7 8.5 %copy-start.2 = (f32[12,96,128]{2,1,0:T(8,128)S(1)}, f32[12,96,128]{2,1,0:T(8,128)}, u32[]{:S(2)}) copy-start(f32[12,96,128]{2,1,0:T(8,128)} %refs_2_.3) | copy-start | bytes 1769476
  0.7 8.5 %copy-start.1 = (f32[12,96,128]{2,1,0:T(8,128)S(1)}, f32[12,96,128]{2,1,0:T(8,128)}, u32[]{:S(2)}) copy-start(f32[12,96,128]{2,1,0:T(8,128)} %refs_1_.3) | copy-start | bytes 1769476
  0.7 8.5 %copy-start = (f32[12,96,128]{2,1,0:T(8,128)S(1)}, f32[12,96,128]{2,1,0:T(8,128)}, u32[]{:S(2)}) copy-start(f32[12,96,128]{2,1,0:T(8,128)} %refs_0_.3) | copy-start | bytes 1769476
  2.6 6.5 %collective-permute-start.16 = (f32[25,8,128]{2,1,0:T(8,128)}, f32[25,8,128]{2,1,0:T(8,128)S(1)}, u32[]{:S(2)}, u32[]{:S(2)}) collective-permute-start(f32[25,8,128]{2,1,0:T(8,128)} %get-tuple-element.19), channel_id=1, source_target_pairs={{0,1},{1,0},{2,3},{3,2},{4,5},{5,4},{6,7},{7,6},{8,9},{9,8},{10,11... | collective-permute-start | bytes 307208 | tf_op jit(solution)/shard_map/ppermute | solution.py:472
  3.7 5.4 %collective-permute-start.3 = (f32[25,8,128]{2,1,0:T(8,128)S(1)}, f32[25,8,128]{2,1,0:T(8,128)}, u32[]{:S(2)}, u32[]{:S(2)}) collective-permute-start(f32[25,8,128]{2,1,0:T(8,128)S(1)} %param.1), channel_id=1, source_target_pairs={{0,4},{1,5},{2,6},{4,0},{5,1},{6,2},{8,12},{9,13},{10,14},{12,8},{... | collective-permute-start | bytes 307208 | tf_op jit(solution)/shard_map/cond/branch_1_fun/ppermute | solution.py:491
  5.3 3.8 %collective-permute-start.2 = (f32[25,8,128]{2,1,0:T(8,128)S(1)}, f32[25,8,128]{2,1,0:T(8,128)}, u32[]{:S(2)}, u32[]{:S(2)}) collective-permute-start(f32[25,8,128]{2,1,0:T(8,128)S(1)} %param.1), channel_id=1, source_target_pairs={{0,4},{4,0},{8,12},{12,8},{16,20},{20,16},{24,28},{28,24},{1,2},{2... | collective-permute-start | bytes 307208 | tf_op jit(solution)/shard_map/cond/branch_1_fun/ppermute | solution.py:490
  11.5 6.5 %collective-permute-start.17 = (f32[28,8,128]{2,1,0:T(8,128)S(1)}, f32[28,8,128]{2,1,0:T(8,128)S(1)}, u32[]{:S(2)}, u32[]{:S(2)}) collective-permute-start(f32[28,8,128]{2,1,0:T(8,128)S(1)} %get-tuple-element.24), channel_id=1, source_target_pairs={{4,0},{8,4},{12,8},{16,12},{20,16},{24,20},{28,24},{0,28},{5,1},{9... | collective-permute-start | bytes 344072 | tf_op jit(solution)/shard_map/ppermute | solution.py:512
  15.6 5.1 %collective-permute-start.18 = (f32[28,8,128]{2,1,0:T(8,128)S(1)}, f32[28,8,128]{2,1,0:T(8,128)S(1)}, u32[]{:S(2)}, u32[]{:S(2)}) collective-permute-start(f32[28,8,128]{2,1,0:T(8,128)S(1)} %get-tuple-element.25), channel_id=1, source_target_pairs={{0,4},{4,8},{8,12},{12,16},{16,20},{20,24},{24,28},{28,0},{1,5},{5... | collective-permute-start | bytes 344072 | tf_op jit(solution)/shard_map/ppermute | solution.py:511
